TPU v7x, 512 devices: a whole 4x8x8 slice. The times are simulated.
512 devices in a mesh: row: 32 (over z, x_hi, core), col: 16 (over x_lo, y).
Axes of the slice: x: 4 (x_hi: 2, x_lo: 2; x = x_hi * 2 + x_lo), y: 8, z: 8, core: 2. Of those that a mesh axis runs over, the one named last changes fastest.
Arguments:
- leg_table: bfloat16 [900, 12288], P(None, ('row', 'col')), may hold values from -5 to 5
- coef_code: int32 [12288], replicated, may hold values from 2 to 601
- colat_idx: int32 [6144], replicated, may hold values from 0 to 899
- lon_idx: int32 [6144], replicated, may hold values from 0 to 3599
- gap_mask: int32 [6144], replicated, may hold values 0 or 1
- obs_weight: float32 [6144], replicated, may hold values from 0.1 to 10
- gradient: float32 [6144], replicated, may hold values from -6 to 6
Outputs:
- normal: float32 [16, 12288, 768], P('col', 'row')
- rhs: float32 [12288], P('row')
Inputs may be any that keep to these rules, and one draw needn't show every extreme that they name: coef_code[c] // 2 is the coefficient's order m and coef_code[c] % 2 is 0 for a cosine and 1 for a sine term.
All inputs are finite; a program needn't handle non-finite values.
Results may differ from a plain program's by a relative error of at most 0.0044.
Values may be sent and summed in bfloat16 or wider, within the bound.
A program may use at most 64 MiB of HBM per device.

v0:
```python
import math

import jax
import jax.numpy as jnp
from jax import lax
from jax.sharding import PartitionSpec as P

NLON = 3600


def synthesize(table, codes, colat_idx, lon_idx):
    rows = jnp.take(table, colat_idx, axis=0).astype(jnp.float32)
    order = codes // 2
    kind = (codes % 2).astype(jnp.float32)
    phase = lon_idx[:, None] * order[None, :] % NLON
    angle = phase.astype(jnp.float32) * (2.0 * math.pi / NLON) - kind[None, :] * (0.5 * math.pi)
    return (rows * jnp.cos(angle)).astype(jnp.bfloat16)


def contract(left_part, right_part):
    return lax.dot_general(
        left_part, right_part, (((0,), (0,)), ((), ())), preferred_element_type=jnp.float32
    )


def shards(leg_table, coef_code, colat_idx, lon_idx, gap_mask, obs_weight, gradient):
    n_col = lax.axis_size("col")
    sub = leg_table.shape[1]
    row_at = lax.axis_index("row")
    col_at = lax.axis_index("col")
    total = colat_idx.shape[0]
    scales = obs_weight * gap_mask.astype(jnp.float32)
    weighted = (scales * gradient).astype(jnp.bfloat16)
    codes_own = lax.dynamic_slice_in_dim(coef_code, (row_at * n_col + col_at) * sub, sub)
    own_design = synthesize(leg_table, codes_own, colat_idx, lon_idx)
    design_row = lax.all_gather(own_design, "col", axis=1, tiled=True)
    left = (design_row.astype(jnp.float32) * scales[:, None]).astype(jnp.bfloat16)
    design_col = lax.all_gather(own_design, "row", axis=1, tiled=True)
    normal = contract(left, design_col) / total
    rhs = jnp.dot(weighted, design_row, preferred_element_type=jnp.float32) / total
    return (normal[None], rhs)


def solution(mesh):
    placed = (P(None, ("row", "col")), P(), P(), P(), P(), P(), P())
    return jax.shard_map(
        shards,
        mesh=mesh,
        in_specs=placed,
        out_specs=(P("col", "row", None), P("row")),
        check_vma=False,
    )
```

profile of v0, /device:TPU:1, one launch (start us, length us, event | category | flops | bytes accessed | tf_op | source)
XLA Modules:
  0.0 248.5 jit_solution(12402000700005669805)
XLA Ops:
  7.2 0.0 all-gather.3.cloned.1.call-start
  7.2 0.8 compare_and_fusion
  8.0 0.7 fusion.13
  8.7 0.8 and_select_fusion.1
  9.5 1.0 copy.13
  10.5 0.0 copy-start
  10.5 0.0 copy-start.1
  10.5 0.0 copy-start.2
  10.5 0.0 copy-start.3
  10.5 18.1 %gather_fusion = bf16[6144,24]{1,0:T(8,128)(2,1)S(1)} fusion(bf16[900,24]{1,0:T(8,128)(2,1)S(1)} %copy.13, s32[6144]{0:T(1024)S(1)} %fusion.13), kind=kCustom, calls=%fused_computation | custom fusion | bytes 614400 | tf_op jit(solution)/shard_map/jit(_take)/gather | solution.py:12
  28.6 0.6 copy.14
  29.3 0.0 copy-done
  29.3 3.1 %fusion.9 = bf16[6144,24]{0,1:T(8,128)(2,1)} fusion(f32[24]{0:T(128)S(1)} %fusion.15, s32[24]{0:T(128)S(1)} %get-tuple-element.4, s32[6144]{0:T(1024)S(1)} %copy-done, bf16[6144,24]{0,1:T(8,128)(2,1)S(1)} %copy.14, pred[6144]{0:T(1024)(128)(4,1)S(1)} %compare_and_fusion), kind=kLoop, calls=%fused_computation.13 | loop fusion | flops 2064384 | bytes 620736 | tf_op jit(solution)/shard_map/convert_element_type | solution.py:17
  32.4 0.0 all-gather.3.cloned.1.call-update
  32.4 0.0 all-gather.5.cloned.1.call-start
  32.5 0.7 all-gather.5.cloned.1.call-update
  33.2 0.0 copy-done.1
  33.2 0.0 copy-done.2
  33.2 0.0 copy-done.3
  33.3 76.1 %all-gather.3.cloned.1.call-done = bf16[6144,384]{0,1:T(8,128)(2,1)} async-done(((bf16[6144,24]{0,1:T(8,128)(2,1)}), bf16[6144,384]{0,1:T(8,128)(2,1)}) %all-gather.3.cloned.1.call-update) | async-done | bytes 4718608 | tf_op jit(solution)/shard_map/all_gather | solution.py:36
  109.3 3.7 %convolution_reduce_fusion = f32[384]{0:T(512)S(1)} fusion(bf16[6144,1]{0,1:T(2,128)(2,1)S(1)} %reshape.23, bf16[6144,384]{0,1:T(8,128)(2,1)} %all-gather.3.cloned.1.call-done), kind=kOutput, calls=%fused_computation.6 | convolution fusion | flops 4718592 | bytes 4732416 | tf_op jit(solution)/shard_map/dot_general | solution.py:40
  113.0 0.6 broadcast_multiply_fusion
  113.6 118.0 %all-gather.5.cloned.1.call-done = bf16[6144,768]{0,1:T(8,128)(2,1)} async-done(((bf16[6144,24]{0,1:T(8,128)(2,1)}), bf16[6144,768]{0,1:T(8,128)(2,1)}) %all-gather.5.cloned.1.call-update) | async-done | bytes 9437200 | tf_op jit(solution)/shard_map/all_gather | solution.py:38
  231.7 10.0 %fusion.3 = f32[1,384,768]{2,1,0:T(8,128)} fusion(bf16[6144,768]{0,1:T(8,128)(2,1)} %all-gather.5.cloned.1.call-done, bf16[6144,384]{0,1:T(8,128)(2,1)} %all-gather.3.cloned.1.call-done, f32[6144]{0:T(1024)S(1)} %get-tuple-element.3), kind=kOutput, calls=%fused_computation.5 | convolution fusion | flops 3631251456 | bytes 15360000 | tf_op jit(solution)/shard_map/dot_general | solution.py:21
  (3 shorter events, 0.0 us)
Async XLA Ops:
  7.2 102.2 %all-gather.3.cloned.1.call-start = ((), (), s32[]{:S(2)}) async-start(), calls=%async_computation | async-start | bytes 5013504 | tf_op jit(solution)/shard_map/all_gather | solution.py:36
  10.5 18.8 %copy-start = (s32[6144]{0:T(1024)S(1)}, s32[6144]{0:T(1024)}, u32[]{:S(2)}) copy-start(s32[6144]{0:T(1024)} %param.10) | copy-start | bytes 73732
  10.5 22.7 %copy-start.1 = (f32[6144]{0:T(1024)S(1)}, f32[6144]{0:T(1024)}, u32[]{:S(2)}) copy-start(f32[6144]{0:T(1024)} %param.13) | copy-start | bytes 73732
  10.5 22.7 %copy-start.2 = (f32[6144]{0:T(1024)S(1)}, f32[6144]{0:T(1024)}, u32[]{:S(2)}) copy-start(f32[6144]{0:T(1024)} %param.12) | copy-start | bytes 73732
  10.5 22.7 %copy-start.3 = (s32[6144]{0:T(1024)S(1)}, s32[6144]{0:T(1024)}, u32[]{:S(2)}) copy-start(s32[6144]{0:T(1024)} %param.11) | copy-start | bytes 73732
  32.4 199.2 %all-gather.5.cloned.1.call-start = ((), (), s32[]{:S(2)}) async-start(), calls=%async_computation.1 | async-start | bytes 9732096 | tf_op jit(solution)/shard_map/all_gather | solution.py:38
Sparse Core Ops, SparseCore 0:
  32.5 76.7 all-gather.2
  113.3 118.3 all-gather.4
where the time goes:
time: 249 us; the launch traced here: 248 us
  waiting for transfers between devices  195 us (78%)
  local copies, waits for them, and re-layouts  19.7 us (8%)
  between operations  14.2 us (6%)
  matrix products  13.7 us (6%)
  other arithmetic  6.03 us (2%)
    all_gather x1, waiting for transfers between devices, shards(): design_col = lax.all_gather(own_design, 'row', axis=1, tiled=True)  118 us
    all_gather x1, waiting for transfers between devices, shards(): design_row = lax.all_gather(own_design, 'col', axis=1, tiled=True)  76.1 us
    gather x2, local copies, waits for them, and re-layouts, synthesize(): rows = jnp.take(table, colat_idx, axis=0).astype(jnp.float32)  18.7 us
    dot_general x1, matrix products, contract(): lax.dot_general(left_part, right_part, (((0,), (0,)), ((), ())), preferre...  9.99 us
  transfers between devices with their start and end apart: 2, of which 2 were waited for; matrix products, arithmetic and copies ran while one was open for 2% of the time, Pallas kernels for 0%

commit v1 on v0

v1 whole, which is shorter than its diff:
```python
import functools

import jax
import jax.numpy as jnp
from jax import lax
from jax.experimental import pallas as pl
from jax.experimental.pallas import tpu as pltpu
from jax.sharding import PartitionSpec as P

NLON = 3600
NTHETA = 900
OBS = 6144
SUB = 24
HALF = OBS // 2
BLOCK = 768
N_BLOCK = HALF // BLOCK
TILE = 384
F32 = jnp.float32
BF16 = jnp.bfloat16
MESH = pl.DeviceIdType.MESH
N_SEND = 66


def sin_turns(w):
    s = w * w
    p = -76.58128455924857 + s * 39.76072207493176
    p = 81.60248074286099 + s * p
    p = -41.341680668063056 + s * p
    p = 6.283185280261415 + s * p
    return w * p


def cos_turns(f):
    return sin_turns(0.25 - jnp.abs(f - jnp.round(f)))


def turns(x):
    return (x - NLON * jnp.round(x * (1.0 / NLON))) * (1.0 / NLON)


def dot(a, b, ca, cb, precision=None):
    return lax.dot_general(
        a, b, (((ca,), (cb,)), ((), ())), preferred_element_type=F32, precision=precision
    )


def kernel(
    leg_ref, code_ref, mask_ref, weight_ref, grad_ref, colat_ref, lon_ref,
    own_ref, rhs_ref, far_ref, far_rhs_ref,
    slots, fold, table, trig, cos_b, sin_b, codes, gathered, s_wide, g_wide,
    total, part, rhs_acc, rhs_part, send_sem, slot_sem, far_sem,
):
    row, col = lax.axis_index("row"), lax.axis_index("col")
    z, h, c = row // 4, (row // 2) % 2, row % 2
    p, y = col // 8, col % 8

    def rid(z_, h_, c_):
        return z_ * 4 + h_ * 2 + c_

    def cid(p_, y_):
        return p_ * 8 + y_

    sib = (rid(z, h, 1 - c), col)
    over_p = (row, cid(1 - p, y))
    over_h = (rid(z, 1 - h, c), col)
    y_up, y_down = (row, cid(p, (y + 1) % 8)), (row, cid(p, (y + 7) % 8))
    z_up, z_down = (rid((z + 1) % 8, h, c), col), (rid((z + 7) % 8, h, c), col)
    peers = (sib, over_p, over_h, y_up, y_down, z_up, z_down)

    barrier = pltpu.get_barrier_semaphore()
    for peer in peers:
        pl.semaphore_signal(barrier, inc=1, device_id=peer, device_id_type=MESH)

    def row_slot(core, plane, y_):
        return core * 16 + plane * 8 + y_

    def col_slot(z_, plane, core):
        return 32 + z_ * 4 + plane * 2 + core

    fold[...] = jnp.zeros_like(fold)
    fold[:, 0:NTHETA] = leg_ref[...].astype(F32)
    own = jnp.concatenate([fold[:, 0:512], fold[:, 512:1024]], axis=0).astype(BF16)
    mine_r, mine_c = row_slot(c, p, y), col_slot(z, h, c)
    slots[mine_r] = own
    slots[mine_c] = own

    started = []

    def copy_of(slot, peer, sem_at):
        return pltpu.make_async_remote_copy(
            src_ref=slots.at[slot], dst_ref=slots.at[slot],
            send_sem=send_sem.at[sem_at], recv_sem=slot_sem.at[slot],
            device_id=peer, device_id_type=MESH,
        )

    def send(slot, peer):
        copy = copy_of(slot, peer, len(started))
        copy.start()
        started.append(copy)

    def arrived(slot):
        copy_of(slot, sib, 0).wait_recv()

    pl.semaphore_wait(barrier, len(peers))

    send(mine_r, y_up)
    send(mine_r, y_down)
    send(mine_c, z_up)
    send(mine_c, z_down)
    send(mine_r, over_p)
    send(mine_c, over_h)
    send(mine_r, sib)
    send(mine_c, sib)

    codes[...] = jnp.zeros_like(codes)
    codes[0, 0:6, :] = code_ref[pl.ds((row // 2) * 6, 6), :].astype(F32)
    lane_at = lax.broadcasted_iota(jnp.int32, (128, 128), 1)
    source_at = lax.broadcasted_iota(jnp.int32, (128, 128), 0)
    all_codes = code_ref[...].astype(F32)
    for k in range(6):
        n = lane_at + k * 128
        i = (n * 2731) >> 16
        place = (i * 16 + col) * SUB + (n - i * SUB)
        pick = (source_at == (place & 127)).astype(F32)
        lanes = dot(all_codes, pick, 1, 0, lax.Precision.HIGHEST)
        keep = source_at[0:96] == (place >> 7)[0:96]
        codes[1, k : k + 1, :] = jnp.sum(jnp.where(keep, lanes, 0.0), axis=0, keepdims=True)
    code = jnp.round(codes[...])
    order = jnp.floor(code * 0.5)
    quarter = (code - 2.0 * order) * 0.25

    @pl.loop(0, 64)
    def _(b):
        angle = turns(order * b.astype(F32))
        cos_b[:, b] = cos_turns(angle)
        sin_b[:, b] = cos_turns(angle - 0.25)

    def trig_part(first, last):
        @pl.loop(first, last)
        def _(a):
            angle = turns(order * (a * 64).astype(F32)) - quarter
            cos_a, sin_a = cos_turns(angle), cos_turns(angle - 0.25)

            @pl.loop(0, 4)
            def _(b4):
                for u in range(16):
                    b = b4 * 16 + u
                    for q in range(2):
                        trig[q, a * 64 + b] = cos_a[q] * cos_b[q, b] - sin_a[q] * sin_b[q, b]

    def wide_part():
        @pl.loop(0, HALF // 128)
        def _(q):
            at = pl.ds(c * (HALF // 128) + q, 1)
            scale = weight_ref[at, :] * mask_ref[at, :].astype(F32)
            rows = pl.ds(pl.multiple_of(q * 128, 128), 128)
            s_wide[rows, :] = jnp.broadcast_to(scale, (128, 128)).T
            g_wide[rows, :] = jnp.broadcast_to(grad_ref[at, :], (128, 128)).T

    trig_part(0, 5)
    slot = row_slot(c, 1 - p, y)
    arrived(slot)
    send(slot, y_up)
    send(slot, y_down)
    send(slot, sib)
    slot = col_slot(z, 1 - h, c)
    arrived(slot)
    send(slot, z_up)
    send(slot, z_down)
    send(slot, sib)

    parts = iter([(5, 10), (10, 17), (17, 24), (24, 31), (31, 38), (38, 46), (46, 57)])
    for step in range(1, 4):
        for half in range(2):
            trig_part(*next(parts))
            if step == 3:
                pr, pc = half, half
            else:
                pr = p if half == 0 else 1 - p
                pc = h if half == 0 else 1 - h
            for up in (True, False):
                forward = step < 3 or (half == 0) == up
                off = 8 - step if up else step
                slot = row_slot(c, pr, (y + off) % 8)
                arrived(slot)
                if forward:
                    send(slot, y_up if up else y_down)
                send(slot, sib)
                slot = col_slot((z + off) % 8, pc, c)
                arrived(slot)
                if forward:
                    send(slot, z_up if up else z_down)
                send(slot, sib)
    trig_part(*next(parts))
    wide_part()
    for half in range(2):
        slot = row_slot(c, half, (y + 4) % 8)
        arrived(slot)
        send(slot, sib)
        slot = col_slot((z + 4) % 8, half, c)
        arrived(slot)
        send(slot, sib)

    @pl.loop(0, 16)
    def _(j):
        arrived((1 - c) * 16 + j)
        arrived(32 + j * 2 + (1 - c))

    eye = (
        lax.broadcasted_iota(jnp.int32, (256, 256), 0)
        == lax.broadcasted_iota(jnp.int32, (256, 256), 1)
    ).astype(BF16)
    flat = table.reshape(2 * 1024 * 8, 128)

    @pl.loop(0, 4)
    def _(group):
        block = slots[pl.ds(group * 16, 16)].astype(F32)
        base = (group // 2) * (1024 * 8) + (group % 2) * 3
        for half in range(2):
            x = block[:, half * SUB : (half + 1) * SUB, :].reshape(TILE, 512).astype(BF16)
            for q in range(2):
                turned = dot(eye, x[:, q * 256 : (q + 1) * 256], 1, 1)
                for k in range(3):
                    first = base + (half * 512 + q * 256) * 8 + k
                    flat[pl.ds(first, 256, stride=8), :] = turned[:, k * 128 : (k + 1) * 128]

    rhs_acc[...] = jnp.zeros_like(rhs_acc)

    def gather(blk):
        first = c * HALF + blk * BLOCK

        @pl.loop(0, BLOCK // 32)
        def _(b):
            at = pl.multiple_of(b * (32 * 12), 8)
            for u in range(32):
                t, l = colat_ref[first + b * 32 + u], lon_ref[first + b * 32 + u]
                gathered[pl.ds(at + u * 12, 8), :] = table[0, t] * trig[0, l]
                gathered[pl.ds(at + u * 12 + 6, 6), :] = (table[1, t] * trig[1, l])[0:6]

    def left_of(blk, half):
        rows = pl.ds(pl.multiple_of(blk * BLOCK, BLOCK), BLOCK)
        s, g = s_wide[rows, :], g_wide[rows, :]
        first = ((1 - c) if half == 0 else c) * 3
        parts = []
        for k in range(3):
            scaled = gathered[pl.ds(first + k, BLOCK, stride=12), :] * s
            rhs_acc[half, k] += jnp.sum((scaled * g).reshape(BLOCK // 8, 8, 128), axis=0)
            parts.append(scaled.astype(BF16))
        return jnp.concatenate(parts, axis=1)

    def right_of():
        return jnp.concatenate(
            [gathered[pl.ds(6 + k, BLOCK, stride=12), :].astype(BF16) for k in range(6)], axis=1
        )

    total[...] = jnp.zeros_like(total)

    @pl.loop(0, N_BLOCK - 1)
    def _(blk):
        gather(blk)
        left = jnp.concatenate([left_of(blk, 0), left_of(blk, 1)], axis=1)
        total[...] += dot(left, right_of(), 0, 0)

    last = N_BLOCK - 1
    gather(last)
    right = right_of()
    part[...] = (total[0:TILE, :] + dot(left_of(last, 0), right, 0, 0)).astype(BF16)
    far = pltpu.make_async_remote_copy(
        src_ref=part, dst_ref=far_ref, send_sem=send_sem.at[N_SEND], recv_sem=far_sem.at[0],
        device_id=sib, device_id_type=MESH,
    )
    far.start()
    own_ref[...] = total[TILE : 2 * TILE, :] + dot(left_of(last, 1), right, 0, 0)
    for k in range(3):
        lanes = slice(k * 128, (k + 1) * 128)
        rhs_part[:, lanes] = jnp.broadcast_to(
            jnp.sum(rhs_acc[0, k], axis=0, keepdims=True), (8, 128)
        )
        rhs_ref[:, lanes] = jnp.broadcast_to(
            jnp.sum(rhs_acc[1, k], axis=0, keepdims=True), (8, 128)
        )
    far_rhs = pltpu.make_async_remote_copy(
        src_ref=rhs_part, dst_ref=far_rhs_ref, send_sem=send_sem.at[N_SEND + 1],
        recv_sem=far_sem.at[1], device_id=sib, device_id_type=MESH,
    )
    far_rhs.start()
    for copy in started:
        copy.wait_send()
    far.wait()
    far_rhs.wait()


def shards(leg_table, coef_code, colat_idx, lon_idx, gap_mask, obs_weight, gradient):
    vmem, smem = pl.BlockSpec(memory_space=pltpu.VMEM), pl.BlockSpec(memory_space=pltpu.SMEM)
    hbm = pl.BlockSpec(memory_space=pl.ANY)
    own, own_rhs, far, far_rhs = pl.pallas_call(
        kernel,
        out_shape=(
            jax.ShapeDtypeStruct((TILE, 768), F32),
            jax.ShapeDtypeStruct((8, TILE), F32),
            jax.ShapeDtypeStruct((TILE, 768), BF16),
            jax.ShapeDtypeStruct((8, TILE), F32),
        ),
        in_specs=[vmem] * 5 + [smem] * 2,
        out_specs=(vmem, vmem, hbm, hbm),
        scratch_shapes=[
            pltpu.VMEM((64, 2 * SUB, 512), BF16),
            pltpu.VMEM((SUB, 1024), F32),
            pltpu.VMEM((2, 1024, 8, 128), F32),
            pltpu.VMEM((2, 57 * 64, 8, 128), F32),
            pltpu.VMEM((2, 64, 8, 128), F32),
            pltpu.VMEM((2, 64, 8, 128), F32),
            pltpu.VMEM((2, 8, 128), F32),
            pltpu.VMEM((BLOCK * 12, 128), F32),
            pltpu.VMEM((HALF, 128), F32),
            pltpu.VMEM((HALF, 128), F32),
            pltpu.VMEM((768, 768), F32),
            pltpu.VMEM((TILE, 768), BF16),
            pltpu.VMEM((2, 3, 8, 128), F32),
            pltpu.VMEM((8, TILE), F32),
            pltpu.SemaphoreType.DMA((N_SEND + 2,)),
            pltpu.SemaphoreType.DMA((64,)),
            pltpu.SemaphoreType.DMA((2,)),
        ],
        compiler_params=pltpu.CompilerParams(
            collective_id=0, has_side_effects=True, vmem_limit_bytes=62 * 2**20
        ),
    )(
        leg_table.T, coef_code.reshape(96, 128), gap_mask.reshape(48, 128),
        obs_weight.reshape(48, 128), gradient.reshape(48, 128), colat_idx, lon_idx,
    )
    normal = (own + far.astype(F32)) * (1.0 / OBS)
    rhs = (own_rhs[0] + far_rhs[0]) * (1.0 / OBS)
    return normal[None], rhs


def solution(mesh):
    placed = (P(None, ("row", "col")), P(), P(), P(), P(), P(), P())
    return jax.shard_map(
        shards,
        mesh=mesh,
        in_specs=placed,
        out_specs=(P("col", "row", None), P("row")),
        check_vma=False,
    )
```

time: 249 us -> 59.5 us (0.24)
  waiting for transfers between devices: 195 us -> 0 us
  Pallas kernels: 0 us -> 54.6 us
  local copies, waits for them, and re-layouts: 19.7 us -> 0 us
  matrix products: 13.7 us -> 0 us
  between operations: 14.2 us -> 0.64 us
    all_gather x2 -> x0, waiting for transfers between devices: 194 us -> none  [the longest x1 118 us: shards(): design_col = lax.all_gather(own_design, 'row', axis=1, tiled=True)]
    pallas_call x0 -> x1, Pallas kernels: none -> 54.6 us  [shards(): pl.pallas_call(kernel, out_shape=(jax.ShapeDtypeStruct((TILE, 768), F32),...]
    gather x2 -> x0, local copies, waits for them, and re-layouts: 18.7 us -> none  [synthesize(): rows = jnp.take(table, colat_idx, axis=0).astype(jnp.float32)]
    dot_general x2 -> x0, matrix products: 13.7 us -> none  [the longest x1 9.99 us: contract(): lax.dot_general(left_part, right_part, (((0,), (0,)), ((), ())), preferre...]
    convert_element_type x2 -> x0, other arithmetic: 3.15 us -> none  [the longest x1 3.14 us: synthesize(): return (rows * jnp.cos(angle)).astype(jnp.bfloat16)]
    broadcast_in_dim x0 -> x1, other arithmetic: none -> 2.57 us  [shards(): return (normal[None], rhs)]
  transfers between devices with their start and end apart: 2 -> 0, of which waited for: 2 -> 0; matrix products, arithmetic and copies ran while one was open for 2% -> 0% of each run, Pallas kernels for 0% -> 0%
where the time goes in v1:
time: 59.5 us; the launch traced here: 59.1 us
  Pallas kernels  54.6 us (92%)
  other arithmetic  3.89 us (7%)
  between operations  0.64 us (1%)
    pallas_call x1, Pallas kernels, shards(): pl.pallas_call(kernel, out_shape=(jax.ShapeDtypeStruct((TILE, 768), F32),...  54.6 us
    broadcast_in_dim x1, other arithmetic, shards(): return (normal[None], rhs)  2.57 us
    mul x1, other arithmetic, shards(): rhs = (own_rhs[0] + far_rhs[0]) * (1.0 / OBS)  1.32 us

profile of v1, /device:TPU:1, one launch (start us, length us, event | category | flops | bytes accessed | tf_op | source)
XLA Modules:
  0.0 59.1 jit_solution(18400606479607424882)
XLA Ops:
  0.6 54.6 %shard_map.86 = (f32[384,768]{1,0:T(8,128)}, f32[8,384]{1,0:T(8,128)}, bf16[384,768]{1,0:T(8,128)(2,1)}, f32[8,384]{1,0:T(8,128)}) custom-call(bf16[24,900]{1,0:T(8,128)(2,1)} %bitcast.7, s32[96,128]{1,0:T(8,128)} %bitcast.8, s32[48,128]{1,0:T(8,128)} %bitcast.9, f32[48,128]{1,0:T(8,128)} %bitcast.10, f32[48,128]{1,0:T(8,128)} %bitcast.11, s32[6144]{0:T(1024)} %colat_ref.1, ...), custom_call_target="tpu_custom_call" | custom-call | tf_op jit(solution)/shard_map/pallas_call | solution.py:296
  55.3 1.3 %multiply_reduce_fusion = f32[384]{0:T(512)} fusion(f32[8,384]{1,0:T(8,128)} %get-tuple-element.9, f32[8,384]{1,0:T(8,128)} %get-tuple-element.8), kind=kLoop, calls=%fused_computation.1 | loop fusion | flops 768 | bytes 4608 | tf_op jit(solution)/shard_map/mul | solution.py:333
  56.6 2.6 %multiply_bitcast_fusion = f32[1,384,768]{2,1,0:T(8,128)} fusion(f32[384,768]{1,0:T(8,128)} %get-tuple-element.6, bf16[384,768]{1,0:T(8,128)(2,1)} %get-tuple-element.7), kind=kLoop, calls=%fused_computation | loop fusion | flops 884736 | bytes 2949120 | tf_op jit(solution)/shard_map/broadcast_in_dim | solution.py:334

commit v2 on v1

v2 whole, which is shorter than its diff:
```python
import functools

import jax
import jax.numpy as jnp
from jax import lax
from jax.experimental import pallas as pl
from jax.experimental.pallas import tpu as pltpu
from jax.sharding import PartitionSpec as P

NLON = 3600
NTHETA = 900
OBS = 6144
SUB = 24
HALF = OBS // 2
BLOCK = 1024
N_BLOCK = HALF // BLOCK
TILE = 384
F32 = jnp.float32
BF16 = jnp.bfloat16
MESH = pl.DeviceIdType.MESH
N_SEND = 62


def sin_turns(w):
    s = w * w
    p = -76.58128455924857 + s * 39.76072207493176
    p = 81.60248074286099 + s * p
    p = -41.341680668063056 + s * p
    p = 6.283185280261415 + s * p
    return w * p


def cos_turns(f):
    return sin_turns(0.25 - jnp.abs(f - jnp.round(f)))


def turns(x):
    return (x - NLON * jnp.round(x * (1.0 / NLON))) * (1.0 / NLON)


def dot(a, b, ca, cb, precision=None):
    return lax.dot_general(
        a, b, (((ca,), (cb,)), ((), ())), preferred_element_type=F32, precision=precision
    )


def kernel(
    leg_hbm, code_hbm, mask_hbm, weight_hbm, grad_hbm, colat_hbm, lon_hbm,
    own_ref, rhs_ref, far_ref, far_rhs_ref,
    slots, leg_ref, fold, table, wave, trig_a, trig_b, codes, gathered,
    total, part, rhs_acc, rhs_part, code_ref, mask_ref, weight_ref, scale_ref, grad_ref, colat_ref, lon_ref,
    send_sem, slot_sem, far_sem, load_sem,
):
    row, col = lax.axis_index("row"), lax.axis_index("col")
    z, h, c = row // 4, (row // 2) % 2, row % 2
    p, y = col // 8, col % 8

    def rid(z_, h_, c_):
        return z_ * 4 + h_ * 2 + c_

    def cid(p_, y_):
        return p_ * 8 + y_

    sib = (rid(z, h, 1 - c), col)
    over_p = (row, cid(1 - p, y))
    over_h = (rid(z, 1 - h, c), col)

    def along_y(off):
        return (row, cid(p, (y + off % 8) % 8))

    def along_z(off):
        return (rid((z + off % 8) % 8, h, c), col)

    near = (1, 2, -1, -2)
    peers = (sib, over_p, over_h) + tuple(along_y(o) for o in near) + tuple(along_z(o) for o in near)

    barrier = pltpu.get_barrier_semaphore()
    for peer in peers:
        pl.semaphore_signal(barrier, inc=1, device_id=peer, device_id_type=MESH)

    my_half = pl.ds(pl.multiple_of(c * HALF, HALF), HALF)
    my_rows = pl.ds(pl.multiple_of(c * (HALF // 128), 8), HALF // 128)
    loads = [
        pltpu.make_async_copy(src, dst, load_sem.at[n])
        for n, (src, dst) in enumerate((
            (leg_hbm, leg_ref), (code_hbm, code_ref), (lon_hbm.at[my_half], lon_ref),
            (colat_hbm.at[my_half], colat_ref), (weight_hbm.at[my_rows], weight_ref),
            (mask_hbm.at[my_rows], mask_ref), (grad_hbm.at[my_half], grad_ref),
        ))
    ]
    for load in loads:
        load.start()

    def row_slot(core, plane, y_):
        return core * 16 + plane * 8 + y_

    def col_slot(z_, plane, core):
        return 32 + z_ * 4 + plane * 2 + core

    fold[...] = jnp.zeros_like(fold)
    loads[0].wait()
    fold[:, 0:NTHETA] = leg_ref[...].astype(F32)
    own = jnp.concatenate([fold[:, 0:512], fold[:, 512:1024]], axis=0).astype(BF16)
    mine_r, mine_c = row_slot(c, p, y), col_slot(z, h, c)
    slots[mine_r] = own
    slots[mine_c] = own

    started = []

    def copy_of(slot, peer, sem_at):
        return pltpu.make_async_remote_copy(
            src_ref=slots.at[slot], dst_ref=slots.at[slot],
            send_sem=send_sem.at[sem_at], recv_sem=slot_sem.at[slot],
            device_id=peer, device_id_type=MESH,
        )

    def send(slot, peer):
        copy = copy_of(slot, peer, len(started))
        copy.start()
        started.append(copy)

    def arrived(slot):
        copy_of(slot, sib, 0).wait_recv()

    pl.semaphore_wait(barrier, len(peers))

    for off in (2, -2):
        send(mine_r, along_y(off))
        send(mine_c, along_z(off))
    send(mine_r, over_p)
    send(mine_c, over_h)
    for off in (1, -1):
        send(mine_r, along_y(off))
        send(mine_c, along_z(off))
    send(mine_r, sib)
    send(mine_c, sib)
    for load in loads[1:]:
        load.wait()
    weight_ref[...] = weight_ref[...] * mask_ref[...].astype(F32)
    to_scalars = pltpu.make_async_copy(weight_ref, scale_ref, load_sem.at[7])
    to_scalars.start()

    codes[...] = jnp.zeros_like(codes)
    codes[0, 0:6, :] = code_ref[pl.ds((row // 2) * 6, 6), :].astype(F32)
    lane_at = lax.broadcasted_iota(jnp.int32, (128, 128), 1)
    source_at = lax.broadcasted_iota(jnp.int32, (128, 128), 0)
    all_codes = code_ref[...].astype(F32)
    for k in range(6):
        n = lane_at + k * 128
        i = (n * 2731) >> 16
        place = (i * 16 + col) * SUB + (n - i * SUB)
        pick = (source_at == (place & 127)).astype(F32)
        lanes = dot(all_codes, pick, 1, 0, lax.Precision.HIGHEST)
        keep = source_at[0:96] == (place >> 7)[0:96]
        codes[1, k : k + 1, :] = jnp.sum(jnp.where(keep, lanes, 0.0), axis=0, keepdims=True)
    code = jnp.round(codes[...])
    order = jnp.floor(code * 0.5)
    quarter = (code - 2.0 * order) * 0.25

    @pl.loop(0, 64)
    def _(n):
        angle = turns(order * n.astype(F32))
        trig_b[n, 0:2] = cos_turns(angle)
        trig_b[n, 2:4] = cos_turns(angle - 0.25)
        angle = turns(order * (n * 64).astype(F32)) - quarter
        trig_a[n, 0:2] = cos_turns(angle)
        trig_a[n, 2:4] = cos_turns(angle - 0.25)

    to_scalars.wait()

    def wave_part(first, last):
        @pl.loop(first // 32, last // 32)
        def _(n):
            lane = (n % 4) * 32
            for u in range(32):
                at = n * 32 + u
                l = lon_ref[at]
                a, b = l >> 6, l & 63
                rows = trig_a[a, 0] * trig_b[b, 0] - trig_a[a, 2] * trig_b[b, 2]
                wave[at, 0] = rows * scale_ref[n // 4, lane + u]
                wave[at, 1] = trig_a[a, 1] * trig_b[b, 1] - trig_a[a, 3] * trig_b[b, 3]

    def row_at(own_plane, off):
        return row_slot(c, p if own_plane else 1 - p, (y + off % 8) % 8)

    def col_at(own_plane, off):
        return col_slot((z + off % 8) % 8, h if own_plane else 1 - h, c)

    ways = ((row_at, along_y), (col_at, along_z))

    def take(slot, *onward):
        arrived(slot)
        for peer in onward:
            send(slot, peer)
        send(slot, sib)

    def second_stage(own_plane):
        for at, along in ways:
            onward = (along(2), along(1)) if own_plane else (along(1),)
            take(at(own_plane, -2), *onward)
        for at, along in ways:
            onward = (along(-1),) if own_plane else (along(-2), along(-1))
            take(at(own_plane, 2), *onward)

    def take_all(own_plane, offs):
        for off in offs:
            for at, _ in ways:
                take(at(own_plane, off))

    for at, along in ways:
        take(at(False, 0), along(2), along(-2), along(1), along(-1))
    wave_part(0, 416)
    second_stage(True)
    wave_part(416, 1376)
    second_stage(False)
    wave_part(1376, 2016)
    take_all(True, (1, -1))
    take_all(False, (1, -1))
    take_all(True, (3, -3, 4))
    wave_part(2016, 3072)
    take_all(False, (3, -3, 4))
    for copy in started[:40]:
        copy.wait_send()

    eye = (
        lax.broadcasted_iota(jnp.int32, (256, 256), 0)
        == lax.broadcasted_iota(jnp.int32, (256, 256), 1)
    ).astype(BF16)
    flat = table.reshape(2 * 1024 * 8, 128)

    def build(group):
        block = slots[pl.ds(group * 16, 16)].astype(F32)
        base = (group // 2) * (1024 * 8) + (group % 2) * 3
        for half in range(2):
            x = block[:, half * SUB : (half + 1) * SUB, :].reshape(TILE, 512).astype(BF16)
            for q in range(2):
                turned = dot(eye, x[:, q * 256 : (q + 1) * 256], 1, 1)
                for k in range(3):
                    first = base + (half * 512 + q * 256) * 8 + k
                    flat[pl.ds(first, 256, stride=8), :] = turned[:, k * 128 : (k + 1) * 128]

    build(c)

    @pl.loop(0, 16)
    def _(j):
        arrived((1 - c) * 16 + j)
        arrived(32 + j * 2 + (1 - c))

    @pl.loop(0, 3)
    def _(n):
        build(jnp.where(n == 0, 1 - c, n + 1))

    rhs_acc[...] = jnp.zeros_like(rhs_acc)

    def gather(blk):
        first = blk * BLOCK

        def some(b, acc):
            at = pl.multiple_of(b * (32 * 12), 8)
            for u in range(32):
                o = first + b * 32 + u
                t = colat_ref[o]
                scaled = table[0, t] * wave[o, 0]
                gathered[pl.ds(at + u * 12, 8), :] = scaled
                gathered[pl.ds(at + u * 12 + 6, 6), :] = (table[1, t] * wave[o, 1])[0:6]
                acc = acc + scaled * grad_ref[o]
            return acc

        rhs_acc[...] = lax.fori_loop(0, BLOCK // 32, some, rhs_acc[...])

    def left_of(half):
        first = ((1 - c) if half == 0 else c) * 3
        return jnp.concatenate(
            [gathered[pl.ds(first + k, BLOCK, stride=12), :].astype(BF16) for k in range(3)], axis=1
        )

    def right_of():
        return jnp.concatenate(
            [gathered[pl.ds(6 + k, BLOCK, stride=12), :].astype(BF16) for k in range(6)], axis=1
        )

    total[...] = jnp.zeros_like(total)

    @pl.loop(0, N_BLOCK - 1)
    def _(blk):
        gather(blk)
        left = jnp.concatenate([left_of(0), left_of(1)], axis=1)
        total[...] += dot(left, right_of(), 0, 0)

    last = N_BLOCK - 1
    gather(last)
    right = right_of()
    part[...] = (total[0:TILE, :] + dot(left_of(0), right, 0, 0)).astype(BF16)
    far = pltpu.make_async_remote_copy(
        src_ref=part, dst_ref=far_ref, send_sem=send_sem.at[N_SEND], recv_sem=far_sem.at[0],
        device_id=sib, device_id_type=MESH,
    )
    far.start()
    total[TILE : 2 * TILE, :] += dot(left_of(1), right, 0, 0)
    near_copy = pltpu.make_async_copy(total.at[pl.ds(TILE, TILE)], own_ref, load_sem.at[0])
    near_copy.start()
    rhs_part[...] = jnp.zeros_like(rhs_part)
    rhs_ref[...] = jnp.zeros_like(rhs_ref)
    rhs_part[0:3, :] = rhs_acc[pl.ds((1 - c) * 3, 3), :]
    rhs_ref[0:3, :] = rhs_acc[pl.ds(c * 3, 3), :]
    far_rhs = pltpu.make_async_remote_copy(
        src_ref=rhs_part, dst_ref=far_rhs_ref, send_sem=send_sem.at[N_SEND + 1],
        recv_sem=far_sem.at[1], device_id=sib, device_id_type=MESH,
    )
    far_rhs.start()
    for copy in started[40:]:
        copy.wait_send()
    near_copy.wait()
    far_rhs.wait()
    far.wait()


def finish(own_ref, rhs_ref, far_ref, far_rhs_ref, normal_ref, sum_ref):
    normal_ref[0] = (own_ref[...] + far_ref[...].astype(F32)) * (1.0 / OBS)

    @pl.when(pl.program_id(0) == 0)
    def _():
        sum_ref[...] = ((rhs_ref[0:3, :] + far_rhs_ref[0:3, :]) * (1.0 / OBS)).reshape(TILE)


def shards(leg_table, coef_code, colat_idx, lon_idx, gap_mask, obs_weight, gradient):
    vmem = pl.BlockSpec(memory_space=pltpu.VMEM)
    hbm = pl.BlockSpec(memory_space=pl.ANY)
    own, own_rhs, far, far_rhs = pl.pallas_call(
        kernel,
        out_shape=(
            jax.ShapeDtypeStruct((TILE, 768), F32),
            jax.ShapeDtypeStruct((8, 128), F32),
            jax.ShapeDtypeStruct((TILE, 768), BF16),
            jax.ShapeDtypeStruct((8, 128), F32),
        ),
        in_specs=[hbm] * 7,
        out_specs=(hbm, vmem, hbm, hbm),
        scratch_shapes=[
            pltpu.VMEM((64, 2 * SUB, 512), BF16),
            pltpu.VMEM((SUB, NTHETA), BF16),
            pltpu.VMEM((SUB, 1024), F32),
            pltpu.VMEM((2, 1024, 8, 128), F32),
            pltpu.VMEM((HALF, 2, 8, 128), F32),
            pltpu.VMEM((64, 4, 8, 128), F32),
            pltpu.VMEM((64, 4, 8, 128), F32),
            pltpu.VMEM((2, 8, 128), F32),
            pltpu.VMEM((BLOCK * 12, 128), F32),
            pltpu.VMEM((768, 768), F32),
            pltpu.VMEM((TILE, 768), BF16),
            pltpu.VMEM((8, 128), F32),
            pltpu.VMEM((8, 128), F32),
            pltpu.VMEM((96, 128), jnp.int32),
            pltpu.VMEM((HALF // 128, 128), jnp.int32),
            pltpu.VMEM((HALF // 128, 128), F32),
            pltpu.SMEM((HALF // 128, 128), F32),
            pltpu.SMEM((HALF,), F32),
            pltpu.SMEM((HALF,), jnp.int32),
            pltpu.SMEM((HALF,), jnp.int32),
            pltpu.SemaphoreType.DMA((N_SEND + 2,)),
            pltpu.SemaphoreType.DMA((64,)),
            pltpu.SemaphoreType.DMA((2,)),
            pltpu.SemaphoreType.DMA((8,)),
        ],
        compiler_params=pltpu.CompilerParams(
            collective_id=0, has_side_effects=True, vmem_limit_bytes=62 * 2**20
        ),
    )(
        leg_table.T, coef_code.reshape(96, 128), gap_mask.reshape(48, 128),
        obs_weight.reshape(48, 128), gradient, colat_idx, lon_idx,
    )
    half = TILE // 2
    normal, rhs = pl.pallas_call(
        finish,
        grid=(2,),
        in_specs=[
            pl.BlockSpec((half, 768), lambda i: (i, 0)),
            pl.BlockSpec((8, 128), lambda i: (0, 0)),
            pl.BlockSpec((half, 768), lambda i: (i, 0)),
            pl.BlockSpec((8, 128), lambda i: (0, 0)),
        ],
        out_specs=(
            pl.BlockSpec((1, half, 768), lambda i: (0, i, 0)),
            pl.BlockSpec((TILE,), lambda i: (0,)),
        ),
        out_shape=(
            jax.ShapeDtypeStruct((1, TILE, 768), F32),
            jax.ShapeDtypeStruct((TILE,), F32),
        ),
    )(own, own_rhs, far, far_rhs)
    return normal, rhs


def solution(mesh):
    placed = (P(None, ("row", "col")), P(), P(), P(), P(), P(), P())
    return jax.shard_map(
        shards,
        mesh=mesh,
        in_specs=placed,
        out_specs=(P("col", "row", None), P("row")),
        check_vma=False,
    )
```

time: 59.5 us -> 50.7 us (0.85)
  Pallas kernels: 54.6 us -> 49.8 us
  other arithmetic: 3.89 us -> 0 us
    pallas_call x1, Pallas kernels: 54.6 us -> 47.5 us  [shards(): pl.pallas_call(kernel, out_shape=(jax.ShapeDtypeStruct((TILE, 768), F32),...]
    broadcast_in_dim x1 -> x0, other arithmetic: 2.57 us -> none  [shards(): return (normal[None], rhs)]
    pallas_call x0 -> x1, Pallas kernels: none -> 2.32 us  [shards(): pl.pallas_call(finish, grid=(2,), in_specs=[pl.BlockSpec((half, 768), lam...]
    mul x1 -> x0, other arithmetic: 1.32 us -> none  [shards(): rhs = (own_rhs[0] + far_rhs[0]) * (1.0 / OBS)]
where the time goes in v2:
time: 50.7 us; the launch traced here: 50.5 us
  Pallas kernels  49.8 us (98%)
  between operations  0.64 us (1%)
    pallas_call x1, Pallas kernels, shards(): pl.pallas_call(kernel, out_shape=(jax.ShapeDtypeStruct((TILE, 768), F32),...  47.5 us
    pallas_call x1, Pallas kernels, shards(): pl.pallas_call(finish, grid=(2,), in_specs=[pl.BlockSpec((half, 768), lam...  2.32 us

profile of v2, /device:TPU:1, one launch (start us, length us, event | category | flops | bytes accessed | tf_op | source)
XLA Modules:
  0.0 50.5 jit_solution(3013681350475871041)
XLA Ops:
  0.6 47.5 %shard_map.86 = (f32[384,768]{1,0:T(8,128)}, f32[8,128]{1,0:T(8,128)}, bf16[384,768]{1,0:T(8,128)(2,1)}, f32[8,128]{1,0:T(8,128)}) custom-call(bf16[24,900]{1,0:T(8,128)(2,1)} %bitcast.4, s32[96,128]{1,0:T(8,128)} %bitcast.5, s32[48,128]{1,0:T(8,128)} %bitcast.6, f32[48,128]{1,0:T(8,128)} %bitcast.7, f32[6144]{0:T(1024)} %grad_hbm.1, s32[6144]{0:T(1024)} %colat_hbm.1, ...), custom_call_target="tpu_custom_call" | custom-call | tf_op jit(solution)/shard_map/pallas_call | solution.py:329
  48.1 2.3 %shard_map.87 = (f32[1,384,768]{2,1,0:T(8,128)}, f32[384]{0:T(512)}) custom-call(f32[384,768]{1,0:T(8,128)} %get-tuple-element.6.own_ref, f32[8,128]{1,0:T(8,128)} %get-tuple-element.7.rhs_ref, bf16[384,768]{1,0:T(8,128)(2,1)} %get-tuple-element.8.far_ref, f32[8,128]{1,0:T(8,128)} %get-tuple-element.9.far_rhs_ref), custom_call_target="tpu_custom_call" | custom-call | tf_op jit(solution)/shard_map/pallas_call | solution.py:373

commit v3 on v2

--- a/solution.py
+++ b/solution.py
@@ -157,27 +157,28 @@
     order = jnp.floor(code * 0.5)
     quarter = (code - 2.0 * order) * 0.25
 
-    @pl.loop(0, 64)
-    def _(n):
-        angle = turns(order * n.astype(F32))
-        trig_b[n, 0:2] = cos_turns(angle)
-        trig_b[n, 2:4] = cos_turns(angle - 0.25)
-        angle = turns(order * (n * 64).astype(F32)) - quarter
-        trig_a[n, 0:2] = cos_turns(angle)
-        trig_a[n, 2:4] = cos_turns(angle - 0.25)
+    @pl.loop(0, 16)
+    def _(n4):
+        for u in range(4):
+            n = n4 * 4 + u
+            angle = turns(order * n.astype(F32))
+            trig_b[n, 0:2] = cos_turns(angle)
+            trig_b[n, 2:4] = cos_turns(angle - 0.25)
+            angle = turns(order * (n * 64).astype(F32)) - quarter
+            trig_a[n, 0:2] = cos_turns(angle)
+            trig_a[n, 2:4] = cos_turns(angle - 0.25)
 
     to_scalars.wait()
 
     def wave_part(first, last):
-        @pl.loop(first // 32, last // 32)
+        @pl.loop(first // 128, last // 128)
         def _(n):
-            lane = (n % 4) * 32
-            for u in range(32):
-                at = n * 32 + u
+            for u in range(128):
+                at = n * 128 + u
                 l = lon_ref[at]
                 a, b = l >> 6, l & 63
                 rows = trig_a[a, 0] * trig_b[b, 0] - trig_a[a, 2] * trig_b[b, 2]
-                wave[at, 0] = rows * scale_ref[n // 4, lane + u]
+                wave[at, 0] = rows * scale_ref[n, u]
                 wave[at, 1] = trig_a[a, 1] * trig_b[b, 1] - trig_a[a, 3] * trig_b[b, 3]
 
     def row_at(own_plane, off):
@@ -209,15 +210,15 @@
 
     for at, along in ways:
         take(at(False, 0), along(2), along(-2), along(1), along(-1))
-    wave_part(0, 416)
+    wave_part(0, 384)
     second_stage(True)
-    wave_part(416, 1376)
+    wave_part(384, 1408)
     second_stage(False)
-    wave_part(1376, 2016)
+    wave_part(1408, 2048)
     take_all(True, (1, -1))
     take_all(False, (1, -1))
     take_all(True, (3, -3, 4))
-    wave_part(2016, 3072)
+    wave_part(2048, 3072)
     take_all(False, (3, -3, 4))
     for copy in started[:40]:
         copy.wait_send()

time: 50.7 us -> 48.6 us (0.959)
  Pallas kernels: 49.8 us -> 47.8 us
    pallas_call x1, Pallas kernels: 47.5 us -> 45.5 us  [shards(): pl.pallas_call(kernel, out_shape=(jax.ShapeDtypeStruct((TILE, 768), F32),...]
where the time goes in v3:
time: 48.6 us; the launch traced here: 48.4 us
  Pallas kernels  47.8 us (98%)
  between operations  0.64 us (1%)
    pallas_call x1, Pallas kernels, shards(): pl.pallas_call(kernel, out_shape=(jax.ShapeDtypeStruct((TILE, 768), F32),...  45.5 us
    pallas_call x1, Pallas kernels, shards(): pl.pallas_call(finish, grid=(2,), in_specs=[pl.BlockSpec((half, 768), lam...  2.32 us

profile of v3, /device:TPU:1, one launch (start us, length us, event | category | flops | bytes accessed | tf_op | source)
XLA Modules:
  0.0 48.4 jit_solution(6281179551521768921)
XLA Ops:
  0.6 45.5 %shard_map.86 = (f32[384,768]{1,0:T(8,128)}, f32[8,128]{1,0:T(8,128)}, bf16[384,768]{1,0:T(8,128)(2,1)}, f32[8,128]{1,0:T(8,128)}) custom-call(bf16[24,900]{1,0:T(8,128)(2,1)} %bitcast.4, s32[96,128]{1,0:T(8,128)} %bitcast.5, s32[48,128]{1,0:T(8,128)} %bitcast.6, f32[48,128]{1,0:T(8,128)} %bitcast.7, f32[6144]{0:T(1024)} %grad_hbm.1, s32[6144]{0:T(1024)} %colat_hbm.1, ...), custom_call_target="tpu_custom_call" | custom-call | tf_op jit(solution)/shard_map/pallas_call | solution.py:330
  46.1 2.3 %shard_map.87 = (f32[1,384,768]{2,1,0:T(8,128)}, f32[384]{0:T(512)}) custom-call(f32[384,768]{1,0:T(8,128)} %get-tuple-element.6.own_ref, f32[8,128]{1,0:T(8,128)} %get-tuple-element.7.rhs_ref, bf16[384,768]{1,0:T(8,128)(2,1)} %get-tuple-element.8.far_ref, f32[8,128]{1,0:T(8,128)} %get-tuple-element.9.far_rhs_ref), custom_call_target="tpu_custom_call" | custom-call | tf_op jit(solution)/shard_map/pallas_call | solution.py:374

commit v4 on v3

--- a/solution.py
+++ b/solution.py
@@ -210,16 +210,17 @@
 
     for at, along in ways:
         take(at(False, 0), along(2), along(-2), along(1), along(-1))
-    wave_part(0, 384)
+    wave_part(0, 512)
     second_stage(True)
-    wave_part(384, 1408)
+    wave_part(512, 1792)
     second_stage(False)
-    wave_part(1408, 2048)
+    wave_part(1792, 2304)
     take_all(True, (1, -1))
     take_all(False, (1, -1))
     take_all(True, (3, -3, 4))
-    wave_part(2048, 3072)
+    wave_part(2304, 3072)
     take_all(False, (3, -3, 4))
+
     for copy in started[:40]:
         copy.wait_send()
 

time: 48.6 us -> 48 us (0.988)
  Pallas kernels: 47.8 us -> 47.1 us
    pallas_call x1, Pallas kernels: 45.5 us -> 44.8 us  [shards(): pl.pallas_call(kernel, out_shape=(jax.ShapeDtypeStruct((TILE, 768), F32),...]
where the time goes in v4:
time: 48 us; the launch traced here: 47.7 us
  Pallas kernels  47.1 us (98%)
  between operations  0.64 us (1%)
    pallas_call x1, Pallas kernels, shards(): pl.pallas_call(kernel, out_shape=(jax.ShapeDtypeStruct((TILE, 768), F32),...  44.8 us
    pallas_call x1, Pallas kernels, shards(): pl.pallas_call(finish, grid=(2,), in_specs=[pl.BlockSpec((half, 768), lam...  2.32 us

profile of v4, /device:TPU:1, one launch (start us, length us, event | category | flops | bytes accessed | tf_op | source)
XLA Modules:
  0.0 47.7 jit_solution(8506817995762951820)
XLA Ops:
  0.6 44.8 %shard_map.86 = (f32[384,768]{1,0:T(8,128)}, f32[8,128]{1,0:T(8,128)}, bf16[384,768]{1,0:T(8,128)(2,1)}, f32[8,128]{1,0:T(8,128)}) custom-call(bf16[24,900]{1,0:T(8,128)(2,1)} %bitcast.4, s32[96,128]{1,0:T(8,128)} %bitcast.5, s32[48,128]{1,0:T(8,128)} %bitcast.6, f32[48,128]{1,0:T(8,128)} %bitcast.7, f32[6144]{0:T(1024)} %grad_hbm.1, s32[6144]{0:T(1024)} %colat_hbm.1, ...), custom_call_target="tpu_custom_call" | custom-call | tf_op jit(solution)/shard_map/pallas_call | solution.py:331
  45.4 2.3 %shard_map.87 = (f32[1,384,768]{2,1,0:T(8,128)}, f32[384]{0:T(512)}) custom-call(f32[384,768]{1,0:T(8,128)} %get-tuple-element.6.own_ref, f32[8,128]{1,0:T(8,128)} %get-tuple-element.7.rhs_ref, bf16[384,768]{1,0:T(8,128)(2,1)} %get-tuple-element.8.far_ref, f32[8,128]{1,0:T(8,128)} %get-tuple-element.9.far_rhs_ref), custom_call_target="tpu_custom_call" | custom-call | tf_op jit(solution)/shard_map/pallas_call | solution.py:375

commit v5 on v4

--- a/solution.py
+++ b/solution.py
@@ -83,7 +83,7 @@
     loads = [
         pltpu.make_async_copy(src, dst, load_sem.at[n])
         for n, (src, dst) in enumerate((
-            (leg_hbm, leg_ref), (code_hbm, code_ref), (lon_hbm.at[my_half], lon_ref),
+            (leg_hbm, leg_ref), (code_hbm, code_ref.at[pl.ds(0, 96)]), (lon_hbm.at[my_half], lon_ref),
             (colat_hbm.at[my_half], colat_ref), (weight_hbm.at[my_rows], weight_ref),
             (mask_hbm.at[my_rows], mask_ref), (grad_hbm.at[my_half], grad_ref),
         ))
@@ -144,7 +144,7 @@
     codes[0, 0:6, :] = code_ref[pl.ds((row // 2) * 6, 6), :].astype(F32)
     lane_at = lax.broadcasted_iota(jnp.int32, (128, 128), 1)
     source_at = lax.broadcasted_iota(jnp.int32, (128, 128), 0)
-    all_codes = code_ref[...].astype(F32)
+    all_codes = code_ref[0:96, :].astype(F32)
     for k in range(6):
         n = lane_at + k * 128
         i = (n * 2731) >> 16
@@ -268,7 +268,7 @@
                 acc = acc + scaled * grad_ref[o]
             return acc
 
-        rhs_acc[...] = lax.fori_loop(0, BLOCK // 32, some, rhs_acc[...])
+        rhs_acc[0:8, :] = lax.fori_loop(0, BLOCK // 32, some, rhs_acc[0:8, :])
 
     def left_of(half):
         first = ((1 - c) if half == 0 else c) * 3
@@ -347,12 +347,12 @@
             pltpu.VMEM((64, 4, 8, 128), F32),
             pltpu.VMEM((64, 4, 8, 128), F32),
             pltpu.VMEM((2, 8, 128), F32),
-            pltpu.VMEM((BLOCK * 12, 128), F32),
+            pltpu.VMEM((BLOCK * 12 + 8, 128), F32),
             pltpu.VMEM((768, 768), F32),
             pltpu.VMEM((TILE, 768), BF16),
+            pltpu.VMEM((16, 128), F32),
             pltpu.VMEM((8, 128), F32),
-            pltpu.VMEM((8, 128), F32),
-            pltpu.VMEM((96, 128), jnp.int32),
+            pltpu.VMEM((104, 128), jnp.int32),
             pltpu.VMEM((HALF // 128, 128), jnp.int32),
             pltpu.VMEM((HALF // 128, 128), F32),
             pltpu.SMEM((HALF // 128, 128), F32),

time: 48 us -> 48 us (level)
  no operation moved by 1% of the time
where the time goes in v5:
time: 48 us; the launch traced here: 47.7 us
  Pallas kernels  47.1 us (98%)
  between operations  0.64 us (1%)
    pallas_call x1, Pallas kernels, shards(): pl.pallas_call(kernel, out_shape=(jax.ShapeDtypeStruct((TILE, 768), F32),...  44.8 us
    pallas_call x1, Pallas kernels, shards(): pl.pallas_call(finish, grid=(2,), in_specs=[pl.BlockSpec((half, 768), lam...  2.32 us

profile of v5, /device:TPU:1, one launch (start us, length us, event | category | flops | bytes accessed | tf_op | source)
XLA Modules:
  0.0 47.7 jit_solution(12715758716854296609)
XLA Ops:
  0.6 44.8 %shard_map.86 = (f32[384,768]{1,0:T(8,128)}, f32[8,128]{1,0:T(8,128)}, bf16[384,768]{1,0:T(8,128)(2,1)}, f32[8,128]{1,0:T(8,128)}) custom-call(bf16[24,900]{1,0:T(8,128)(2,1)} %bitcast.4, s32[96,128]{1,0:T(8,128)} %bitcast.5, s32[48,128]{1,0:T(8,128)} %bitcast.6, f32[48,128]{1,0:T(8,128)} %bitcast.7, f32[6144]{0:T(1024)} %grad_hbm.1, s32[6144]{0:T(1024)} %colat_hbm.1, ...), custom_call_target="tpu_custom_call" | custom-call | tf_op jit(solution)/shard_map/pallas_call | solution.py:331
  45.4 2.3 %shard_map.87 = (f32[1,384,768]{2,1,0:T(8,128)}, f32[384]{0:T(512)}) custom-call(f32[384,768]{1,0:T(8,128)} %get-tuple-element.6.own_ref, f32[8,128]{1,0:T(8,128)} %get-tuple-element.7.rhs_ref, bf16[384,768]{1,0:T(8,128)(2,1)} %get-tuple-element.8.far_ref, f32[8,128]{1,0:T(8,128)} %get-tuple-element.9.far_rhs_ref), custom_call_target="tpu_custom_call" | custom-call | tf_op jit(solution)/shard_map/pallas_call | solution.py:375
